TPU v7x, 32 devices: a whole 2x2x4 slice. The times are simulated.
32 devices in a mesh: slot: 4 (over y, x), row: 8 (over z, core).
Axes of the slice: x: 2, y: 2, z: 4, core: 2. Of those that a mesh axis runs over, the one named last changes fastest.
Arguments:
- innovation: bfloat16 [4, 3, 1408, 1408], P('slot', None, 'row'), may hold values from -6 to 6
- clear_mask: int32 [4, 3, 1408, 1408], P('slot', None, 'row'), may hold values 0 or 1
- lag_list: int32 [4], replicated, may hold values from 0 to 3, as said below
Outputs:
- cross_spectra: float32 [2, 4, 3, 1408, 1408], P(None, None, None, 'slot', 'row')
Inputs may be any that keep to these rules, and one draw needn't show every extreme that they name: `lag_list`: both 0 and 3 appear in every list; entries may repeat.
All inputs are finite; a program needn't handle non-finite values. No bound on the sum of `clear_mask` on one device may be relied on, other than what follows from the above.
Results may differ from a plain program's by a relative error of at most 0.009.
Values may be sent and summed in bfloat16 or wider, within the bound.
A program may use at most 512 MiB of HBM per device.

v0:
```python
import math

import jax
import jax.numpy as jnp
from jax import lax
from jax.sharding import PartitionSpec as P


def from_behind(value, axis, steps):
    count = lax.axis_size(axis)
    first, last = (max(0, -steps), min(count, count - steps))
    return lax.ppermute(value, axis, [(source, source + steps) for source in range(first, last)])


def tables(length):
    indices = jnp.arange(length, dtype=jnp.int32)
    phases = indices[:, None] * indices[None, :] % length
    angles = phases.astype(jnp.float32) * (2.0 * math.pi / length)
    norm_scale = 1.0 / math.sqrt(length)
    return (
        (jnp.cos(angles) * norm_scale).astype(jnp.bfloat16),
        (jnp.sin(angles) * norm_scale).astype(jnp.bfloat16),
    )


def cross_term(earlier, later):
    early_wide = earlier.astype(jnp.float32)
    late_wide = later.astype(jnp.float32)
    pair_real = (early_wide[0] * late_wide[0] + early_wide[1] * late_wide[1]).astype(jnp.bfloat16)
    pair_imag = (early_wide[1] * late_wide[0] - early_wide[0] * late_wide[1]).astype(jnp.bfloat16)
    return jnp.stack([pair_real, pair_imag])


def on_device(innovation, clear_mask, lag_list):
    masked = innovation[0] * clear_mask[0].astype(jnp.bfloat16)
    rows_here = masked.shape[1]
    col_count = masked.shape[2]
    cosine_cols, sine_cols = tables(col_count)
    cosine_rows, sine_rows = tables(rows_here * lax.axis_size("row"))
    pieces = []
    for channel in range(masked.shape[0]):
        channel_block = masked[channel : channel + 1]
        flattened = channel_block.reshape(-1, col_count)
        g_real = jnp.dot(flattened, cosine_cols, preferred_element_type=jnp.float32).astype(
            jnp.bfloat16
        )
        g_imag = (-jnp.dot(flattened, sine_cols, preferred_element_type=jnp.float32)).astype(
            jnp.bfloat16
        )
        channel_block = jnp.stack([g_real, g_imag]).reshape(
            2, channel_block.shape[0], rows_here, col_count
        )
        gathered = lax.all_to_all(channel_block, "row", split_axis=3, concat_axis=2, tiled=True)
        real_part = gathered[0]
        imag_part = gathered[1]
        f_real = jnp.einsum(
            "kr,crq->ckq", cosine_rows, real_part, preferred_element_type=jnp.float32
        ) + jnp.einsum("kr,crq->ckq", sine_rows, imag_part, preferred_element_type=jnp.float32)
        f_imag = jnp.einsum(
            "kr,crq->ckq", cosine_rows, imag_part, preferred_element_type=jnp.float32
        ) - jnp.einsum("kr,crq->ckq", sine_rows, real_part, preferred_element_type=jnp.float32)
        pieces.append(jnp.stack([f_real, f_imag]).astype(jnp.bfloat16))
    spectra = jnp.concatenate(pieces, axis=1)
    slot_count = lax.axis_size("slot")
    counts = (slot_count - lag_list).astype(jnp.float32)
    products = [cross_term(spectra, spectra)]
    passed = spectra
    for distance in range(1, slot_count):
        passed = from_behind(passed, "slot", 1)
        products.append(cross_term(passed, spectra))
    stacked = jnp.stack(products)
    selector = (lag_list[:, None] == jnp.arange(slot_count, dtype=jnp.int32)[None, :]).astype(
        jnp.bfloat16
    )
    partial_value = jnp.einsum(
        "lk,kxcrq->xlcrq", selector, stacked, preferred_element_type=jnp.float32
    )
    summed = lax.psum_scatter(
        partial_value.astype(jnp.bfloat16), "slot", scatter_dimension=3, tiled=True
    ).astype(jnp.float32)
    return summed / counts[None, :, None, None, None]


def solution(mesh):
    placed = (P("slot", None, "row", None), P("slot", None, "row", None), P())
    return jax.shard_map(
        on_device,
        mesh=mesh,
        in_specs=placed,
        out_specs=P(None, None, None, "slot", "row"),
        check_vma=False,
    )
```

profile of v0, /device:TPU:0, one launch (start us, length us, event | category | flops | bytes accessed | tf_op | source)
XLA Modules:
  0.0 2325.9 jit_solution(15933230161288131455)
XLA Ops:
  9.1 32.2 %fusion.48 = bf16[1,176,1408]{2,1,0:T(8,128)(2,1)S(1)} fusion(bf16[1,3,176,1408]{3,2,1,0:T(8,128)(2,1)S(1)} %convert_multiply_fusion), kind=kOutput, calls=%fused_computation.68 | convolution fusion | flops 719882240 | bytes 991232 | tf_op jit(solution)/shard_map/dot_general | solution.py:44
  41.3 32.4 %fusion.49 = bf16[1,176,1408]{2,1,0:T(8,128)(2,1)S(1)} fusion(bf16[1,3,176,1408]{3,2,1,0:T(8,128)(2,1)S(1)} %convert_multiply_fusion), kind=kOutput, calls=%fused_computation.69 | convolution fusion | flops 720130048 | bytes 991232 | tf_op jit(solution)/shard_map/dot_general | solution.py:47
  76.7 6.5 all-to-all-start
  83.2 33.2 %fusion.47 = bf16[1,176,1408]{2,1,0:T(8,128)(2,1)S(1)} fusion(bf16[1,3,176,1408]{3,2,1,0:T(8,128)(2,1)} %copy-done), kind=kOutput, calls=%fused_computation.67 | convolution fusion | flops 719882240 | bytes 991232 | tf_op jit(solution)/shard_map/dot_general | solution.py:44
  116.4 33.4 %fusion.50 = bf16[1,176,1408]{2,1,0:T(8,128)(2,1)S(1)} fusion(bf16[1,3,176,1408]{3,2,1,0:T(8,128)(2,1)} %copy-done), kind=kOutput, calls=%fused_computation.70 | convolution fusion | flops 720130048 | bytes 991232 | tf_op jit(solution)/shard_map/dot_general | solution.py:47
  152.9 33.2 %fusion.46 = bf16[1,176,1408]{2,1,0:T(8,128)(2,1)S(1)} fusion(bf16[1,3,176,1408]{3,2,1,0:T(8,128)(2,1)} %copy-done), kind=kOutput, calls=%fused_computation.66 | convolution fusion | flops 719882240 | bytes 991232 | tf_op jit(solution)/shard_map/dot_general | solution.py:44
  186.1 33.4 %fusion.51 = bf16[1,176,1408]{2,1,0:T(8,128)(2,1)S(1)} fusion(bf16[1,3,176,1408]{3,2,1,0:T(8,128)(2,1)} %copy-done), kind=kOutput, calls=%fused_computation.71 | convolution fusion | flops 720130048 | bytes 991232 | tf_op jit(solution)/shard_map/dot_general | solution.py:47
  222.5 5.5 all-to-all-start.1
  229.7 33.0 %fusion.14 = f32[176,1408]{1,0:T(8,128)} fusion(bf16[1408,176]{0,1:T(8,128)(2,1)S(1)} %reshape.216), kind=kOutput, calls=%fused_computation.21 | convolution fusion | flops 719634432 | bytes 1486848 | tf_op jit(solution)/shard_map/kr,crq->ckq/dot_general | solution.py:56
  263.4 32.4 %fusion.13 = f32[176,1408]{1,0:T(8,128)S(1)} fusion(bf16[1408,176]{0,1:T(8,128)(2,1)S(1)} %reshape.217), kind=kOutput, calls=%fused_computation.20 | convolution fusion | flops 719634432 | bytes 1486848 | tf_op jit(solution)/shard_map/kr,crq->ckq/dot_general | solution.py:59
  295.8 32.4 %fusion.52 = bf16[1,1,1408,176]{2,3,1,0:T(8,128)(2,1)S(1)} fusion(f32[176,1408]{1,0:T(8,128)S(1)} %copy-done.9, bf16[1408,176]{0,1:T(8,128)(2,1)S(1)} %reshape.217), kind=kOutput, calls=%fused_computation.72 | convolution fusion | flops 720130048 | bytes 1982464 | tf_op jit(solution)/shard_map/kr,crq->ckq/dot_general | solution.py:58
  328.2 33.5 %fusion.53 = bf16[1,1,1408,176]{2,3,1,0:T(8,128)(2,1)} fusion(f32[176,1408]{1,0:T(8,128)S(1)} %fusion.13, bf16[1408,176]{0,1:T(8,128)(2,1)S(1)} %copy-done.5), kind=kOutput, calls=%fused_computation.73 | convolution fusion | flops 720130048 | bytes 1982464 | tf_op jit(solution)/shard_map/kr,crq->ckq/dot_general | solution.py:61
  361.6 5.1 all-to-all-start.2
  369.2 34.0 %fusion.11 = f32[176,1408]{1,0:T(8,128)} fusion(bf16[1408,176]{0,1:T(8,128)(2,1)} %reshape.220), kind=kOutput, calls=%fused_computation.18 | convolution fusion | flops 719634432 | bytes 1486848 | tf_op jit(solution)/shard_map/kr,crq->ckq/dot_general | solution.py:56
  403.9 32.4 %fusion.10 = f32[176,1408]{1,0:T(8,128)S(1)} fusion(bf16[1408,176]{0,1:T(8,128)(2,1)S(1)} %reshape.221), kind=kOutput, calls=%fused_computation.17 | convolution fusion | flops 719634432 | bytes 1486848 | tf_op jit(solution)/shard_map/kr,crq->ckq/dot_general | solution.py:59
  436.3 33.0 %fusion.54 = bf16[1,1,1408,176]{2,3,1,0:T(8,128)(2,1)} fusion(f32[176,1408]{1,0:T(8,128)S(1)} %copy-done.10, bf16[1408,176]{0,1:T(8,128)(2,1)S(1)} %reshape.221), kind=kOutput, calls=%fused_computation.74 | convolution fusion | flops 720130048 | bytes 1982464 | tf_op jit(solution)/shard_map/kr,crq->ckq/dot_general | solution.py:58
  469.3 33.5 %fusion.55 = bf16[1,1,1408,176]{2,3,1,0:T(8,128)(2,1)} fusion(f32[176,1408]{1,0:T(8,128)S(1)} %fusion.10, bf16[1408,176]{0,1:T(8,128)(2,1)S(1)} %copy-done.6), kind=kOutput, calls=%fused_computation.75 | convolution fusion | flops 720130048 | bytes 1982464 | tf_op jit(solution)/shard_map/kr,crq->ckq/dot_general | solution.py:61
  504.3 32.4 %fusion.8 = f32[176,1408]{1,0:T(8,128)S(1)} fusion(bf16[1408,176]{0,1:T(8,128)(2,1)S(1)} %reshape.224), kind=kOutput, calls=%fused_computation.15 | convolution fusion | flops 719634432 | bytes 1486848 | tf_op jit(solution)/shard_map/kr,crq->ckq/dot_general | solution.py:56
  537.4 32.4 %fusion.7 = f32[176,1408]{1,0:T(8,128)S(1)} fusion(bf16[1408,176]{0,1:T(8,128)(2,1)S(1)} %reshape.225), kind=kOutput, calls=%fused_computation.14 | convolution fusion | flops 719634432 | bytes 1486848 | tf_op jit(solution)/shard_map/kr,crq->ckq/dot_general | solution.py:59
  569.8 32.8 %fusion.56 = bf16[1,1,1408,176]{2,3,1,0:T(8,128)(2,1)S(1)} fusion(f32[176,1408]{1,0:T(8,128)S(1)} %fusion.8, bf16[1408,176]{0,1:T(8,128)(2,1)S(1)} %reshape.225), kind=kOutput, calls=%fused_computation.76 | convolution fusion | flops 720130048 | bytes 1982464 | tf_op jit(solution)/shard_map/kr,crq->ckq/dot_general | solution.py:58
  602.6 32.8 %fusion.57 = bf16[1,1,1408,176]{2,3,1,0:T(8,128)(2,1)S(1)} fusion(f32[176,1408]{1,0:T(8,128)S(1)} %fusion.7, bf16[1408,176]{0,1:T(8,128)(2,1)S(1)} %reshape.224), kind=kOutput, calls=%fused_computation.77 | convolution fusion | flops 720130048 | bytes 1982464 | tf_op jit(solution)/shard_map/kr,crq->ckq/dot_general | solution.py:61
  639.7 64.1 %collective-permute-done = bf16[2,3,1408,176]{2,3,1,0:T(8,128)(2,1)S(1)} collective-permute-done((bf16[2,3,1408,176]{2,3,1,0:T(8,128)(2,1)S(1)}, bf16[2,3,1408,176]{2,3,1,0:T(8,128)(2,1)S(1)}, u32[]{:S(2)}, u32[]{:S(2)}) %collective-permute-start) | collective-permute-done | bytes 2973728 | tf_op jit(solution)/shard_map/ppermute | solution.py:12
  703.8 4.6 collective-permute-start.1
  708.4 63.3 %collective-permute-done.1 = bf16[2,3,1408,176]{2,3,1,0:T(8,128)(2,1)S(1)} collective-permute-done((bf16[2,3,1408,176]{2,3,1,0:T(8,128)(2,1)S(1)}, bf16[2,3,1408,176]{2,3,1,0:T(8,128)(2,1)S(1)}, u32[]{:S(2)}, u32[]{:S(2)}) %collective-permute-start.1) | collective-permute-done | bytes 2973728 | tf_op jit(solution)/shard_map/ppermute | solution.py:12
  771.7 6.0 collective-permute-start.2
  781.0 57.7 %collective-permute-done.2 = bf16[2,3,1408,176]{2,3,1,0:T(8,128)(2,1)} collective-permute-done((bf16[2,3,1408,176]{2,3,1,0:T(8,128)(2,1)S(1)}, bf16[2,3,1408,176]{2,3,1,0:T(8,128)(2,1)}, u32[]{:S(2)}, u32[]{:S(2)}) %collective-permute-start.2) | collective-permute-done | bytes 2973728 | tf_op jit(solution)/shard_map/ppermute | solution.py:12
  845.7 16.2 fusion
  861.8 288.2 %copy.28 = bf16[2,4,3,1408,176]{1,4,2,0,3:T(8,128)(2,1)} copy(bf16[2,4,3,1408,176]{3,1,4,2,0:T(4,128)(2,1)} %fusion) | data formatting | bytes 23789568
  1150.1 746.2 %reshape.227 = bf16[1408,4224]{1,0:T(8,128)(2,1)} reshape(bf16[1408,2,3,176,4]{4,3,2,1,0:T(8,128)(2,1)} %bitcast.44) | data formatting | bytes 23789568
  1896.9 118.5 %reduce-scatter.4.cloned.1.call-done = bf16[352,4224]{1,0:T(8,128)(2,1)} async-done(((bf16[1408,4224]{1,0:T(8,128)(2,1)}), bf16[352,4224]{1,0:T(8,128)(2,1)}) %reduce-scatter.4.cloned.1.call-update) | async-done | bytes 2973712
  2015.4 203.8 %reshape.228 = bf16[352,2,3,176,4]{4,3,2,1,0:T(8,128)(2,1)} reshape(bf16[352,4224]{1,0:T(8,128)(2,1)} %reduce-scatter.4.cloned.1.call-done) | data formatting | bytes 5947392
  2219.3 96.2 %copy.26 = bf16[2,4,3,352,176]{3,4,2,1,0:T(8,128)(2,1)S(1)} copy(bf16[2,4,3,352,176]{1,4,2,0,3:T(8,128)(2,1)} %bitcast.45) | data formatting | bytes 5947392 | tf_op jit(solution)/shard_map/reduce_scatter | solution.py:78
  (58 shorter events, 37.7 us)
Async XLA Ops:
  9.1 32.2 %copy-start = (bf16[1,3,176,1408]{3,2,1,0:T(8,128)(2,1)}, bf16[1,3,176,1408]{3,2,1,0:T(8,128)(2,1)S(1)}, u32[]{:S(2)}) copy-start(bf16[1,3,176,1408]{3,2,1,0:T(8,128)(2,1)S(1)} %convert_multiply_fusion) | copy-start | bytes 4460548
  76.7 145.8 %all-to-all-start = ((bf16[2,1,176,1408]{2,0,1,3:T(2,128)(2,1)}), bf16[2,1,176,1408]{2,0,1,3:T(2,128)(2,1)S(1)}, u32[]{:S(2)}, u32[]{:S(2)}) async-start(bf16[2,1,176,1408]{2,0,1,3:T(2,128)(2,1)} %copy.19), calls=%async_computation | async-start | bytes 2883584 | tf_op jit(solution)/shard_map/all_to_all | solution.py:53
  222.5 139.1 %all-to-all-start.1 = ((bf16[2,1,176,1408]{2,0,1,3:T(2,128)(2,1)}), bf16[2,1,176,1408]{2,0,1,3:T(2,128)(2,1)S(1)}, u32[]{:S(2)}, u32[]{:S(2)}) async-start(bf16[2,1,176,1408]{2,0,1,3:T(2,128)(2,1)} %copy.21), calls=%async_computation.1 | async-start | bytes 2883584 | tf_op jit(solution)/shard_map/all_to_all | solution.py:53
  229.7 33.0 %copy-start.4 = (bf16[1408,176]{0,1:T(8,128)(2,1)}, bf16[1408,176]{0,1:T(8,128)(2,1)S(1)}, u32[]{:S(2)}) copy-start(bf16[1408,176]{0,1:T(8,128)(2,1)S(1)} %reshape.216) | copy-start | bytes 1486852
  263.4 32.4 %copy-start.9 = (f32[176,1408]{1,0:T(8,128)S(1)}, f32[176,1408]{1,0:T(8,128)}, u32[]{:S(2)}) copy-start(f32[176,1408]{1,0:T(8,128)} %fusion.14) | copy-start | bytes 2973700
  295.8 32.4 %copy-start.5 = (bf16[1408,176]{0,1:T(8,128)(2,1)S(1)}, bf16[1408,176]{0,1:T(8,128)(2,1)}, u32[]{:S(2)}) copy-start(bf16[1408,176]{0,1:T(8,128)(2,1)} %copy-done.4) | copy-start | bytes 1486852
  361.6 141.1 %all-to-all-start.2 = ((bf16[2,1,176,1408]{2,0,1,3:T(2,128)(2,1)}), bf16[2,1,176,1408]{2,0,1,3:T(2,128)(2,1)S(1)}, u32[]{:S(2)}, u32[]{:S(2)}) async-start(bf16[2,1,176,1408]{2,0,1,3:T(2,128)(2,1)} %copy.23), calls=%async_computation.2 | async-start | bytes 2883584 | tf_op jit(solution)/shard_map/all_to_all | solution.py:53
  366.7 1648.7 %reduce-scatter.4.cloned.1.call-start = ((), (), s32[]{:S(2)}) async-start(), calls=%async_computation.4 | async-start | bytes 14868480
  403.9 32.4 %copy-start.10 = (f32[176,1408]{1,0:T(8,128)S(1)}, f32[176,1408]{1,0:T(8,128)}, u32[]{:S(2)}) copy-start(f32[176,1408]{1,0:T(8,128)} %fusion.11) | copy-start | bytes 2973700
  436.3 33.0 %copy-start.6 = (bf16[1408,176]{0,1:T(8,128)(2,1)S(1)}, bf16[1408,176]{0,1:T(8,128)(2,1)}, u32[]{:S(2)}) copy-start(bf16[1408,176]{0,1:T(8,128)(2,1)} %reshape.220) | copy-start | bytes 1486852
  602.6 32.9 %copy-start.1 = (bf16[1,1,1408,176]{2,3,1,0:T(8,128)(2,1)S(1)}, bf16[1,1,1408,176]{2,3,1,0:T(8,128)(2,1)}, u32[]{:S(2)}) copy-start(bf16[1,1,1408,176]{2,3,1,0:T(8,128)(2,1)} %fusion.53) | copy-start | bytes 1486852
  602.6 32.9 %copy-start.2 = (bf16[1,1,1408,176]{2,3,1,0:T(8,128)(2,1)S(1)}, bf16[1,1,1408,176]{2,3,1,0:T(8,128)(2,1)}, u32[]{:S(2)}) copy-start(bf16[1,1,1408,176]{2,3,1,0:T(8,128)(2,1)} %fusion.54) | copy-start | bytes 1486852
  602.6 32.9 %copy-start.3 = (bf16[1,1,1408,176]{2,3,1,0:T(8,128)(2,1)S(1)}, bf16[1,1,1408,176]{2,3,1,0:T(8,128)(2,1)}, u32[]{:S(2)}) copy-start(bf16[1,1,1408,176]{2,3,1,0:T(8,128)(2,1)} %fusion.55) | copy-start | bytes 1486852
  636.1 67.7 %collective-permute-start = (bf16[2,3,1408,176]{2,3,1,0:T(8,128)(2,1)S(1)}, bf16[2,3,1408,176]{2,3,1,0:T(8,128)(2,1)S(1)}, u32[]{:S(2)}, u32[]{:S(2)}) collective-permute-start(bf16[2,3,1408,176]{2,3,1,0:T(8,128)(2,1)S(1)} %get-tuple-element.16), channel_id=1, source_target_pairs={{0,8},{8,16},{16,24},{1,9},{9,17},{17,25},{2,10},{10,18},{18,26},{... | collective-permute-start | bytes 8921096 | tf_op jit(solution)/shard_map/ppermute | solution.py:12
  703.8 67.9 %collective-permute-start.1 = (bf16[2,3,1408,176]{2,3,1,0:T(8,128)(2,1)S(1)}, bf16[2,3,1408,176]{2,3,1,0:T(8,128)(2,1)S(1)}, u32[]{:S(2)}, u32[]{:S(2)}) collective-permute-start(bf16[2,3,1408,176]{2,3,1,0:T(8,128)(2,1)S(1)} %collective-permute-done), channel_id=1, source_target_pairs={{0,8},{8,16},{16,24},{1,9},{9,17},{17,25},{2,10},{10,18},{18,26},{... | collective-permute-start | bytes 8921096 | tf_op jit(solution)/shard_map/ppermute | solution.py:12
  771.7 67.0 %collective-permute-start.2 = (bf16[2,3,1408,176]{2,3,1,0:T(8,128)(2,1)S(1)}, bf16[2,3,1408,176]{2,3,1,0:T(8,128)(2,1)}, u32[]{:S(2)}, u32[]{:S(2)}) collective-permute-start(bf16[2,3,1408,176]{2,3,1,0:T(8,128)(2,1)S(1)} %collective-permute-done.1), channel_id=1, source_target_pairs={{0,8},{8,16},{16,24},{1,9},{9,17},{17,25},{2,10},{10,18},{18,26},{... | collective-permute-start | bytes 8921096 | tf_op jit(solution)/shard_map/ppermute | solution.py:12
  843.8 1.9 copy-start.7
  1896.3 0.7 copy-start.8
Sparse Core Ops, SparseCore 0:
  1896.4 118.9 reduce-scatter.3
where the time goes:
time: 2350 us; the launch traced here: 2330 us
  local copies, waits for them, and re-layouts  1350 us (57%)
  matrix products  608 us (26%)
  waiting for transfers between devices  304 us (13%)
  starting transfers between devices  31.3 us (1%)
    unnamed x25, local copies, waits for them, and re-layouts  1240 us
    ppermute x3, waiting for transfers between devices, from_behind(): lax.ppermute(value, axis, [(source, source + steps) for source in range(f...  185 us
    unnamed x2, waiting for transfers between devices  119 us
    dot_general x3, matrix products, on_device(): jnp.einsum('kr,crq->ckq', sine_rows, real_part, preferred_element_type=jn...  99.8 us
    dot_general x3, matrix products, on_device(): jnp.einsum('kr,crq->ckq', cosine_rows, real_part, preferred_element_type=...  99.4 us
    dot_general x3, matrix products, on_device(): jnp.dot(flattened, sine_cols, preferred_element_type=jnp.float32)  99.2 us
    dot_general x3, matrix products, on_device(): jnp.dot(flattened, cosine_cols, preferred_element_type=jnp.float32)  98.5 us
    dot_general x3, matrix products, on_device(): jnp.einsum('kr,crq->ckq', sine_rows, imag_part, preferred_element_type=jn...  98.1 us
  transfers between devices with their start and end apart: 7, of which 4 were waited for; matrix products, arithmetic and copies ran while one was open for 18% of the time, Pallas kernels for 0%

commit v1 on v0

v1 whole, which is shorter than its diff:
```python
import math

import jax
import jax.numpy as jnp
import ml_dtypes
import numpy as np
from jax import lax
from jax.sharding import PartitionSpec as P


def tables(length):
    indices = np.arange(length, dtype=np.int64)
    phases = indices[:, None] * indices[None, :] % length
    angles = phases.astype(np.float32) * np.float32(2.0 * math.pi / length)
    norm_scale = np.float32(1.0 / math.sqrt(length))
    return np.cos(angles) * norm_scale, np.sin(angles) * norm_scale


def column_table(length, parts):
    cosine, sine = tables(length)
    both = np.stack([cosine, -sine]).reshape(2, length, parts, length // parts)
    both = both.transpose(2, 0, 1, 3).reshape(parts * 2, length, length // parts)
    return np.ascontiguousarray(both).astype(ml_dtypes.bfloat16)


def row_table(length, parts, slots):
    cosine, sine = tables(length)
    both = np.stack([np.stack([cosine, sine]), np.stack([-sine, cosine])])
    both = both.reshape(2, 2, slots, length // slots, parts, length // parts)
    both = both.transpose(2, 0, 3, 4, 1, 5).reshape(2 * slots, length // slots, 2 * length)
    return np.ascontiguousarray(both).astype(ml_dtypes.bfloat16)


def on_device(innovation, clear_mask, lag_list):
    masked = innovation[0] * clear_mask[0].astype(jnp.bfloat16)
    channels, rows_here, col_count = masked.shape
    row_parts = lax.axis_size("row")
    slot_count = lax.axis_size("slot")
    rows = rows_here * row_parts
    cols_here = col_count // row_parts
    to_columns = jnp.asarray(column_table(col_count, row_parts))
    to_rows = jnp.asarray(row_table(rows, row_parts, slot_count))
    distances = []
    for channel in range(channels):
        spread = jnp.broadcast_to(masked[channel], (2 * row_parts, rows_here, col_count))
        g = lax.dot_general(
            spread,
            to_columns,
            (((2,), (1,)), ((0,), (0,))),
            preferred_element_type=jnp.float32,
        ).astype(jnp.bfloat16)
        g = g.reshape(row_parts, 2, rows_here, cols_here)
        g = lax.all_to_all(g, "row", split_axis=0, concat_axis=0, tiled=True)
        g = jnp.broadcast_to(
            g.reshape(2 * rows, cols_here), (2 * slot_count, 2 * rows, cols_here)
        )
        f = lax.dot_general(
            to_rows,
            g,
            (((2,), (1,)), ((0,), (0,))),
            preferred_element_type=jnp.float32,
        ).astype(jnp.bfloat16)
        f = f.reshape(slot_count, 2, rows // slot_count, cols_here)
        f = lax.all_to_all(f, "slot", split_axis=0, concat_axis=0, tiled=True)
        wide = f.astype(jnp.float32)
        sums = []
        for distance in range(slot_count):
            real = imag = 0.0
            for at in range(slot_count - distance):
                early, late = wide[at], wide[at + distance]
                pair_real = early[0] * late[0] + early[1] * late[1]
                pair_imag = early[1] * late[0] - early[0] * late[1]
                real = real + pair_real.astype(jnp.bfloat16).astype(jnp.float32)
                imag = imag + pair_imag.astype(jnp.bfloat16).astype(jnp.float32)
            weight = 1.0 / (slot_count - distance)
            sums.append((real * weight, imag * weight))
        distances.append(lax.optimization_barrier(sums))
    parts = []
    for part in range(2):
        entries = []
        for entry in range(lag_list.shape[0]):
            for channel in range(channels):
                chosen = distances[channel][0][part]
                for distance in range(1, slot_count):
                    chosen = jnp.where(
                        lag_list[entry] == distance, distances[channel][distance][part], chosen
                    )
                entries.append(chosen)
        parts.extend(entries)
    return jnp.stack(parts).reshape(2, lag_list.shape[0], channels, rows // slot_count, cols_here)


def solution(mesh):
    placed = (P("slot", None, "row", None), P("slot", None, "row", None), P())
    return jax.shard_map(
        on_device,
        mesh=mesh,
        in_specs=placed,
        out_specs=P(None, None, None, "slot", "row"),
        check_vma=False,
    )
```

time: 2350 us -> 188 us (0.08)
  local copies, waits for them, and re-layouts: 1350 us -> 10.5 us
  matrix products: 608 us -> 48.2 us
  waiting for transfers between devices: 304 us -> 82.3 us
    unnamed x25 -> x30, local copies, waits for them, and re-layouts: 1240 us -> 5.06 us
    dot_general x19 -> x6, matrix products: 608 us -> 48.2 us  [the longest x3 31.1 us: on_device(): lax.dot_general(to_rows, g, (((2,), (1,)), ((0,), (0,))), preferred_eleme...]
    ppermute x3 -> x0, waiting for transfers between devices: 185 us -> none  [from_behind(): lax.ppermute(value, axis, [(source, source + steps) for source in range(f...]
    unnamed x2 -> x0, waiting for transfers between devices: 119 us -> none
    reduce_scatter x1 -> x0, local copies, waits for them, and re-layouts: 96.2 us -> none  [on_device(): lax.psum_scatter(partial_value.astype(jnp.bfloat16), 'slot', scatter_dime...]
    all_to_all x3 -> x6, waiting for transfers between devices: 0.01 us -> 82.3 us  [the longest x3 69.8 us: on_device(): g = lax.all_to_all(g, 'row', split_axis=0, concat_axis=0, tiled=True)]
  transfers between devices with their start and end apart: 7 -> 6, of which waited for: 4 -> 5; matrix products, arithmetic and copies ran while one was open for 18% -> 30% of each run, Pallas kernels for 0% -> 0%
where the time goes in v1:
time: 188 us; the launch traced here: 187 us
  waiting for transfers between devices  82.3 us (44%)
  matrix products  48.2 us (26%)
  starting transfers between devices  25.8 us (14%)
  other arithmetic  12.6 us (7%)
  local copies, waits for them, and re-layouts  10.5 us (6%)
  between operations  7.86 us (4%)
    all_to_all x3, waiting for transfers between devices, on_device(): g = lax.all_to_all(g, 'row', split_axis=0, concat_axis=0, tiled=True)  69.8 us
    dot_general x3, matrix products, on_device(): lax.dot_general(to_rows, g, (((2,), (1,)), ((0,), (0,))), preferred_eleme...  31.1 us
    dot_general x3, matrix products, on_device(): lax.dot_general(spread, to_columns, (((2,), (1,)), ((0,), (0,))), preferr...  17.2 us
    all_to_all x3, starting transfers between devices, on_device(): g = lax.all_to_all(g, 'row', split_axis=0, concat_axis=0, tiled=True)  14.2 us
    all_to_all x3, waiting for transfers between devices, on_device(): f = lax.all_to_all(f, 'slot', split_axis=0, concat_axis=0, tiled=True)  12.5 us
    all_to_all x3, starting transfers between devices, on_device(): f = lax.all_to_all(f, 'slot', split_axis=0, concat_axis=0, tiled=True)  11.7 us
    unnamed x30, local copies, waits for them, and re-layouts  5.06 us
    mul x9, other arithmetic, on_device(): sums.append((real * weight, imag * weight))  4.82 us
  transfers between devices with their start and end apart: 6, of which 5 were waited for; matrix products, arithmetic and copies ran while one was open for 30% of the time, Pallas kernels for 0%

profile of v1, /device:TPU:0, one launch (start us, length us, event | category | flops | bytes accessed | tf_op | source)
XLA Modules:
  0.0 187.3 jit_solution(17477272380645797094)
XLA Ops:
  0.0 2.7 %convert_multiply_fusion = bf16[1,3,176,1408]{3,2,1,0:T(8,128)(2,1)S(1)} fusion(bf16[1,3,176,1408]{3,2,1,0:T(8,128)(2,1)} %param.5, s32[1,3,176,1408]{3,2,1,0:T(8,128)} %param.6), kind=kLoop, calls=%fused_computation.18 | loop fusion | flops 1486848 | bytes 5947392 | tf_op jit(solution)/shard_map/mul | solution.py:35
  2.8 1.8 copy-done.14
  4.6 3.6 %fusion.18 = bf16[16,176,176]{2,1,0:T(8,128)(2,1)} fusion(bf16[16,1408,176]{1,2,0:T(8,128)(2,1)S(1)} %copy-done.14, bf16[176,1408]{1,0:T(8,128)(2,1)S(1)} %get-tuple-element.74), kind=kOutput, calls=%fused_computation.14 | convolution fusion | flops 1396150272 | bytes 9416704 | tf_op jit(solution)/shard_map/dot_general | solution.py:46
  8.2 6.3 %all-to-all-start.4 = ((bf16[8,2,176,176]{3,2,1,0:T(8,128)(2,1)}), bf16[8,2,176,176]{3,2,1,0:T(8,128)(2,1)S(1)}, u32[]{:S(2)}, u32[]{:S(2)}) async-start(bf16[8,2,176,176]{3,2,1,0:T(8,128)(2,1)} %bitcast.32), calls=%async_computation.4 | async-start | bytes 2883584 | tf_op jit(solution)/shard_map/all_to_all | solution.py:53
  14.5 6.8 %fusion.15 = bf16[16,176,176]{2,1,0:T(8,128)(2,1)} fusion(bf16[16,1408,176]{1,2,0:T(8,128)(2,1)} %constant.28.clone, bf16[176,1408]{1,0:T(8,128)(2,1)S(1)} %get-tuple-element.75), kind=kOutput, calls=%fused_computation.13 | convolution fusion | flops 1396150272 | bytes 9416704 | tf_op jit(solution)/shard_map/dot_general | solution.py:46
  21.3 28.2 %all-to-all-done.4 = bf16[8,2,176,176]{3,2,1,0:T(8,128)(2,1)S(1)} async-done(((bf16[8,2,176,176]{3,2,1,0:T(8,128)(2,1)}), bf16[8,2,176,176]{3,2,1,0:T(8,128)(2,1)S(1)}, u32[]{:S(2)}, u32[]{:S(2)}) %all-to-all-start.4) | async-done | bytes 991264 | tf_op jit(solution)/shard_map/all_to_all | solution.py:53
  49.5 3.6 %all-to-all-start.2 = ((bf16[8,2,176,176]{3,2,1,0:T(8,128)(2,1)}), bf16[8,2,176,176]{3,2,1,0:T(8,128)(2,1)S(1)}, u32[]{:S(2)}, u32[]{:S(2)}) async-start(bf16[8,2,176,176]{3,2,1,0:T(8,128)(2,1)} %bitcast.157), calls=%async_computation.2 | async-start | bytes 2883584 | tf_op jit(solution)/shard_map/all_to_all | solution.py:53
  53.1 6.8 %fusion.12 = bf16[16,176,176]{2,1,0:T(8,128)(2,1)} fusion(bf16[16,1408,176]{1,2,0:T(8,128)(2,1)} %constant.28.clone, bf16[176,1408]{1,0:T(8,128)(2,1)S(1)} %get-tuple-element.76), kind=kOutput, calls=%fused_computation.12 | convolution fusion | flops 1396150272 | bytes 9416704 | tf_op jit(solution)/shard_map/dot_general | solution.py:46
  59.9 28.2 %all-to-all-done.2 = bf16[8,2,176,176]{3,2,1,0:T(8,128)(2,1)S(1)} async-done(((bf16[8,2,176,176]{3,2,1,0:T(8,128)(2,1)}), bf16[8,2,176,176]{3,2,1,0:T(8,128)(2,1)S(1)}, u32[]{:S(2)}, u32[]{:S(2)}) %all-to-all-start.2) | async-done | bytes 991264 | tf_op jit(solution)/shard_map/all_to_all | solution.py:53
  88.0 4.3 %all-to-all-start = ((bf16[8,2,176,176]{3,2,1,0:T(8,128)(2,1)}), bf16[8,2,176,176]{3,2,1,0:T(8,128)(2,1)}, u32[]{:S(2)}, u32[]{:S(2)}) async-start(bf16[8,2,176,176]{3,2,1,0:T(8,128)(2,1)} %bitcast.156), calls=%async_computation | async-start | bytes 2883584 | tf_op jit(solution)/shard_map/all_to_all | solution.py:53
  92.3 0.7 fusion.42
  100.6 1.5 copy.8
  102.0 1.5 copy.7
  103.5 10.4 %fusion.27 = bf16[8,176,352]{2,1,0:T(8,128)(2,1)} fusion(bf16[8,352,2816]{2,1,0:T(8,128)(2,1)} %constant.29.clone, bf16[2816,176]{0,1:T(8,128)(2,1)} %copy.8), kind=kOutput, calls=%fused_computation.17 | convolution fusion | flops 2791804928 | bytes 17842176 | tf_op jit(solution)/shard_map/dot_general | solution.py:57
  113.9 13.5 %all-to-all-done = bf16[8,2,176,176]{3,2,1,0:T(8,128)(2,1)} async-done(((bf16[8,2,176,176]{3,2,1,0:T(8,128)(2,1)}), bf16[8,2,176,176]{3,2,1,0:T(8,128)(2,1)}, u32[]{:S(2)}, u32[]{:S(2)}) %all-to-all-start) | async-done | bytes 991264 | tf_op jit(solution)/shard_map/all_to_all | solution.py:53
  127.3 3.7 %all-to-all-start.5 = ((bf16[4,2,352,176]{2,3,1,0:T(8,128)(2,1)}), bf16[4,2,352,176]{2,3,1,0:T(8,128)(2,1)S(1)}, u32[]{:S(2)}, u32[]{:S(2)}) async-start(bf16[4,2,352,176]{2,3,1,0:T(8,128)(2,1)} %bitcast.35), calls=%async_computation.5 | async-start | bytes 2162688 | tf_op jit(solution)/shard_map/all_to_all | solution.py:64
  131.1 1.7 copy.6
  132.8 10.4 %fusion.21 = bf16[8,176,352]{2,1,0:T(8,128)(2,1)} fusion(bf16[8,352,2816]{2,1,0:T(8,128)(2,1)} %constant.29.clone, bf16[2816,176]{0,1:T(8,128)(2,1)S(1)} %copy.6), kind=kOutput, calls=%fused_computation.15 | convolution fusion | flops 2791804928 | bytes 17842176 | tf_op jit(solution)/shard_map/dot_general | solution.py:57
  143.2 1.7 all-to-all-done.5
  144.9 3.7 %all-to-all-start.1 = ((bf16[4,2,352,176]{2,3,1,0:T(8,128)(2,1)}), bf16[4,2,352,176]{2,3,1,0:T(8,128)(2,1)S(1)}, u32[]{:S(2)}, u32[]{:S(2)}) async-start(bf16[4,2,352,176]{2,3,1,0:T(8,128)(2,1)} %bitcast.5), calls=%async_computation.1 | async-start | bytes 2162688 | tf_op jit(solution)/shard_map/all_to_all | solution.py:64
  148.6 10.3 %fusion.24 = bf16[8,176,352]{2,1,0:T(8,128)(2,1)} fusion(bf16[8,352,2816]{2,1,0:T(8,128)(2,1)} %constant.29.clone, bf16[2816,176]{0,1:T(8,128)(2,1)S(1)} %copy-done.11), kind=kOutput, calls=%fused_computation.16 | convolution fusion | flops 2791804928 | bytes 17842176 | tf_op jit(solution)/shard_map/dot_general | solution.py:57
  158.9 1.4 convert_element_type.772
  160.3 1.1 multiply_bitcast_fusion.7
  161.3 1.0 multiply_bitcast_fusion.13
  162.3 4.2 %all-to-all-start.3 = ((bf16[4,2,352,176]{2,3,1,0:T(8,128)(2,1)}), bf16[4,2,352,176]{2,3,1,0:T(8,128)(2,1)}, u32[]{:S(2)}, u32[]{:S(2)}) async-start(bf16[4,2,352,176]{2,3,1,0:T(8,128)(2,1)} %bitcast.158), calls=%async_computation.3 | async-start | bytes 2162688 | tf_op jit(solution)/shard_map/all_to_all | solution.py:64
  166.7 1.0 multiply_bitcast_fusion.11
  167.8 1.0 multiply_bitcast_fusion.17
  169.3 10.8 %all-to-all-done.3 = bf16[4,2,352,176]{2,3,1,0:T(8,128)(2,1)} async-done(((bf16[4,2,352,176]{2,3,1,0:T(8,128)(2,1)}), bf16[4,2,352,176]{2,3,1,0:T(8,128)(2,1)}, u32[]{:S(2)}, u32[]{:S(2)}) %all-to-all-start.3) | async-done | bytes 991264 | tf_op jit(solution)/shard_map/all_to_all | solution.py:64
  180.1 1.4 convert_element_type.708
  181.6 0.2 multiply_bitcast_fusion.9
  183.4 0.2 copy-done.1
  184.6 2.8 %copy-done.12 = f32[24,352,176]{1,2,0:T(8,128)} copy-done((f32[24,352,176]{1,2,0:T(8,128)}, f32[24,352,176]{1,2,0:T(8,128)S(1)}, u32[]{:S(2)}) %copy-start.12) | copy-done | bytes 5947416
  (61 shorter events, 3.2 us)
Async XLA Ops:
  0.0 4.6 %copy-start.14 = (bf16[16,1408,176]{1,2,0:T(8,128)(2,1)S(1)}, bf16[16,1408,176]{1,2,0:T(8,128)(2,1)}, u32[]{:S(2)}) copy-start(bf16[16,1408,176]{1,2,0:T(8,128)(2,1)} %constant.28.clone) | copy-start | bytes 23789572
  8.2 41.4 %all-to-all-start.4 = ((bf16[8,2,176,176]{3,2,1,0:T(8,128)(2,1)}), bf16[8,2,176,176]{3,2,1,0:T(8,128)(2,1)S(1)}, u32[]{:S(2)}, u32[]{:S(2)}) async-start(bf16[8,2,176,176]{3,2,1,0:T(8,128)(2,1)} %bitcast.32), calls=%async_computation.4 | async-start | bytes 2883584 | tf_op jit(solution)/shard_map/all_to_all | solution.py:53
  49.5 38.5 %all-to-all-start.2 = ((bf16[8,2,176,176]{3,2,1,0:T(8,128)(2,1)}), bf16[8,2,176,176]{3,2,1,0:T(8,128)(2,1)S(1)}, u32[]{:S(2)}, u32[]{:S(2)}) async-start(bf16[8,2,176,176]{3,2,1,0:T(8,128)(2,1)} %bitcast.157), calls=%async_computation.2 | async-start | bytes 2883584 | tf_op jit(solution)/shard_map/all_to_all | solution.py:53
  53.1 39.2 %copy-start.13 = (s32[4]{0:T(128)S(1)}, s32[4]{0:T(128)}, u32[]{:S(2)}) copy-start(s32[4]{0:T(128)} %param.7) | copy-start | bytes 52
  88.0 39.3 %all-to-all-start = ((bf16[8,2,176,176]{3,2,1,0:T(8,128)(2,1)}), bf16[8,2,176,176]{3,2,1,0:T(8,128)(2,1)}, u32[]{:S(2)}, u32[]{:S(2)}) async-start(bf16[8,2,176,176]{3,2,1,0:T(8,128)(2,1)} %bitcast.156), calls=%async_computation | async-start | bytes 2883584 | tf_op jit(solution)/shard_map/all_to_all | solution.py:53
  127.3 17.6 %all-to-all-start.5 = ((bf16[4,2,352,176]{2,3,1,0:T(8,128)(2,1)}), bf16[4,2,352,176]{2,3,1,0:T(8,128)(2,1)S(1)}, u32[]{:S(2)}, u32[]{:S(2)}) async-start(bf16[4,2,352,176]{2,3,1,0:T(8,128)(2,1)} %bitcast.35), calls=%async_computation.5 | async-start | bytes 2162688 | tf_op jit(solution)/shard_map/all_to_all | solution.py:64
  132.8 15.9 %copy-start.11 = (bf16[2816,176]{0,1:T(8,128)(2,1)S(1)}, bf16[2816,176]{0,1:T(8,128)(2,1)}, u32[]{:S(2)}) copy-start(bf16[2816,176]{0,1:T(8,128)(2,1)} %copy.7) | copy-start | bytes 2973700
  144.9 3.7 %copy-start.10 = (bf16[4,2,352,176]{2,3,1,0:T(8,128)(2,1)}, bf16[4,2,352,176]{2,3,1,0:T(8,128)(2,1)S(1)}, u32[]{:S(2)}) copy-start(bf16[4,2,352,176]{2,3,1,0:T(8,128)(2,1)S(1)} %all-to-all-done.5) | copy-start | bytes 2973700
  144.9 17.4 %all-to-all-start.1 = ((bf16[4,2,352,176]{2,3,1,0:T(8,128)(2,1)}), bf16[4,2,352,176]{2,3,1,0:T(8,128)(2,1)S(1)}, u32[]{:S(2)}, u32[]{:S(2)}) async-start(bf16[4,2,352,176]{2,3,1,0:T(8,128)(2,1)} %bitcast.5), calls=%async_computation.1 | async-start | bytes 2162688 | tf_op jit(solution)/shard_map/all_to_all | solution.py:64
  162.3 17.7 %all-to-all-start.3 = ((bf16[4,2,352,176]{2,3,1,0:T(8,128)(2,1)}), bf16[4,2,352,176]{2,3,1,0:T(8,128)(2,1)}, u32[]{:S(2)}, u32[]{:S(2)}) async-start(bf16[4,2,352,176]{2,3,1,0:T(8,128)(2,1)} %bitcast.158), calls=%async_computation.3 | async-start | bytes 2162688 | tf_op jit(solution)/shard_map/all_to_all | solution.py:64
  169.2 13.0 %copy-start.5 = (f32[352,176]{0,1:T(8,128)S(1)}, f32[352,176]{0,1:T(8,128)}, u32[]{:S(2)}) copy-start(f32[352,176]{0,1:T(8,128)} %get-tuple-element.31) | copy-start | bytes 743428
  169.3 13.0 %copy-start.7 = (f32[352,176]{0,1:T(8,128)S(1)}, f32[352,176]{0,1:T(8,128)}, u32[]{:S(2)}) copy-start(f32[352,176]{0,1:T(8,128)} %get-tuple-element.32) | copy-start | bytes 743428
  180.1 2.2 %copy-start.9 = (f32[352,176]{0,1:T(8,128)S(1)}, f32[352,176]{0,1:T(8,128)}, u32[]{:S(2)}) copy-start(f32[352,176]{0,1:T(8,128)} %get-tuple-element.30) | copy-start | bytes 743428
  181.5 1.0 copy-start.2
  181.5 1.0 copy-start.3
  181.5 1.1 copy-start.4
  181.6 1.1 copy-start.8
  181.9 1.1 copy-start.6
  182.6 1.0 copy-start.1
  182.8 1.0 copy-start
  184.5 2.8 %copy-start.12 = (f32[24,352,176]{1,2,0:T(8,128)}, f32[24,352,176]{1,2,0:T(8,128)S(1)}, u32[]{:S(2)}) copy-start(f32[24,352,176]{1,2,0:T(8,128)S(1)} %bitcast_dynamic-update-slice_fusion) | copy-start | bytes 17842180

commit v2 on v1

--- a/solution.py
+++ b/solution.py
@@ -19,16 +19,32 @@
 def column_table(length, parts):
     cosine, sine = tables(length)
     both = np.stack([cosine, -sine]).reshape(2, length, parts, length // parts)
-    both = both.transpose(2, 0, 1, 3).reshape(parts * 2, length, length // parts)
+    both = both.transpose(2, 1, 0, 3).reshape(parts, length, 2 * (length // parts))
     return np.ascontiguousarray(both).astype(ml_dtypes.bfloat16)
 
 
 def row_table(length, parts, slots):
     cosine, sine = tables(length)
     both = np.stack([np.stack([cosine, sine]), np.stack([-sine, cosine])])
-    both = both.reshape(2, 2, slots, length // slots, parts, length // parts)
-    both = both.transpose(2, 0, 3, 4, 1, 5).reshape(2 * slots, length // slots, 2 * length)
+    both = both.reshape(2, 2, slots, length // slots, length)
+    both = both.transpose(2, 0, 3, 1, 4).reshape(2 * slots, length // slots, 2 * length)
     return np.ascontiguousarray(both).astype(ml_dtypes.bfloat16)
+
+
+def to_slot_owners(spectrum, count):
+    here = lax.axis_index("slot")
+    blocks = spectrum
+    for step in range(1, count):
+        if count & (count - 1) == 0:
+            pairs = [(at, at ^ step) for at in range(count)]
+            target = source = here ^ step
+        else:
+            pairs = [(at, (at + step) % count) for at in range(count)]
+            target, source = (here + step) % count, (here - step) % count
+        block = lax.dynamic_index_in_dim(spectrum, target, 0, keepdims=True)
+        arrived = lax.ppermute(block, "slot", pairs)
+        blocks = lax.dynamic_update_slice_in_dim(blocks, arrived, source, 0)
+    return blocks
 
 
 def on_device(innovation, clear_mask, lag_list):
@@ -40,28 +56,36 @@
     cols_here = col_count // row_parts
     to_columns = jnp.asarray(column_table(col_count, row_parts))
     to_rows = jnp.asarray(row_table(rows, row_parts, slot_count))
-    distances = []
+    columns = []
     for channel in range(channels):
-        spread = jnp.broadcast_to(masked[channel], (2 * row_parts, rows_here, col_count))
-        g = lax.dot_general(
-            spread,
-            to_columns,
-            (((2,), (1,)), ((0,), (0,))),
-            preferred_element_type=jnp.float32,
-        ).astype(jnp.bfloat16)
-        g = g.reshape(row_parts, 2, rows_here, cols_here)
+        spread = jnp.broadcast_to(masked[channel], (row_parts, rows_here, col_count))
+        columns.append(
+            lax.dot_general(
+                spread,
+                to_columns,
+                (((2,), (1,)), ((0,), (0,))),
+                preferred_element_type=jnp.float32,
+            ).astype(jnp.bfloat16)
+        )
+    spectra = []
+    for channel in range(channels):
+        g = columns[channel]
+        if channel >= 2:
+            g, spectra[channel - 2] = lax.optimization_barrier((g, spectra[channel - 2]))
         g = lax.all_to_all(g, "row", split_axis=0, concat_axis=0, tiled=True)
-        g = jnp.broadcast_to(
-            g.reshape(2 * rows, cols_here), (2 * slot_count, 2 * rows, cols_here)
-        )
+        g = g.reshape(rows, 2 * cols_here)
+        g = jnp.concatenate([g[:, :cols_here], g[:, cols_here:]], axis=0)
+        g = jnp.broadcast_to(g, (2 * slot_count, 2 * rows, cols_here))
         f = lax.dot_general(
             to_rows,
             g,
             (((2,), (1,)), ((0,), (0,))),
             preferred_element_type=jnp.float32,
         ).astype(jnp.bfloat16)
-        f = f.reshape(slot_count, 2, rows // slot_count, cols_here)
-        f = lax.all_to_all(f, "slot", split_axis=0, concat_axis=0, tiled=True)
+        spectra.append(f.reshape(slot_count, 2, rows // slot_count, cols_here))
+    distances = []
+    for channel in range(channels):
+        f = to_slot_owners(spectra[channel], slot_count)
         wide = f.astype(jnp.float32)
         sums = []
         for distance in range(slot_count):

time: 188 us -> 171 us (0.910)
  waiting for transfers between devices: 82.3 us -> 62.3 us
  local copies, waits for them, and re-layouts: 10.5 us -> 16.8 us
    all_to_all x3, waiting for transfers between devices: 69.8 us -> 28.4 us  [on_device(): g = lax.all_to_all(g, 'row', split_axis=0, concat_axis=0, tiled=True)]
    ppermute x0 -> x9, waiting for transfers between devices: none -> 33.9 us  [to_slot_owners(): arrived = lax.ppermute(block, 'slot', pairs)]
    all_to_all x3 -> x0, waiting for transfers between devices: 12.5 us -> none  [on_device(): f = lax.all_to_all(f, 'slot', split_axis=0, concat_axis=0, tiled=True)]
    all_to_all x3 -> x0, starting transfers between devices: 11.7 us -> none  [on_device(): f = lax.all_to_all(f, 'slot', split_axis=0, concat_axis=0, tiled=True)]
    ppermute x0 -> x9, starting transfers between devices: none -> 10.8 us  [to_slot_owners(): arrived = lax.ppermute(block, 'slot', pairs)]
    concatenate x0 -> x3, local copies, waits for them, and re-layouts: none -> 5.64 us  [on_device(): g = jnp.concatenate([g[:, :cols_here], g[:, cols_here:]], axis=0)]
    reshape x3 -> x0, local copies, waits for them, and re-layouts: 4.61 us -> none  [on_device(): g.reshape(2 * rows, cols_here)]
    concatenate x0 -> x3, other arithmetic: none -> 2.91 us  [on_device(): g = jnp.concatenate([g[:, :cols_here], g[:, cols_here:]], axis=0)]
  transfers between devices with their start and end apart: 6 -> 12, of which waited for: 5 -> 7; matrix products, arithmetic and copies ran while one was open for 30% -> 26% of each run, Pallas kernels for 0% -> 0%
where the time goes in v2:
time: 171 us
  waiting for transfers between devices  62.3 us (36%)
  matrix products  46.5 us (27%)
  starting transfers between devices  25.4 us (15%)
  local copies, waits for them, and re-layouts  16.8 us (10%)
  other arithmetic  11.4 us (7%)
  between operations  8.22 us (5%)
    ppermute x9, waiting for transfers between devices, to_slot_owners(): arrived = lax.ppermute(block, 'slot', pairs)  33.9 us
    all_to_all x3, waiting for transfers between devices, on_device(): g = lax.all_to_all(g, 'row', split_axis=0, concat_axis=0, tiled=True)  28.4 us
    dot_general x3, matrix products, on_device(): lax.dot_general(to_rows, g, (((2,), (1,)), ((0,), (0,))), preferred_eleme...  28.2 us
    dot_general x3, matrix products, on_device(): lax.dot_general(spread, to_columns, (((2,), (1,)), ((0,), (0,))), preferr...  18.3 us
    all_to_all x3, starting transfers between devices, on_device(): g = lax.all_to_all(g, 'row', split_axis=0, concat_axis=0, tiled=True)  14.5 us
    ppermute x9, starting transfers between devices, to_slot_owners(): arrived = lax.ppermute(block, 'slot', pairs)  10.8 us
    concatenate x3, local copies, waits for them, and re-layouts, on_device(): g = jnp.concatenate([g[:, :cols_here], g[:, cols_here:]], axis=0)  5.64 us
    unnamed x16, local copies, waits for them, and re-layouts  5.47 us
  transfers between devices with their start and end apart: 12, of which 7 were waited for; matrix products, arithmetic and copies ran while one was open for 26% of the time, Pallas kernels for 0%

profile of v2, /device:TPU:0, one launch (start us, length us, event | category | flops | bytes accessed | tf_op | source)
XLA Modules:
  0.0 170.8 jit_solution(1477319803604413864)
XLA Ops:
  0.0 2.7 %convert_multiply_fusion = bf16[1,3,176,1408]{3,2,1,0:T(8,128)(2,1)S(1)} fusion(bf16[1,3,176,1408]{3,2,1,0:T(8,128)(2,1)} %param.5, s32[1,3,176,1408]{3,2,1,0:T(8,128)} %param.6), kind=kLoop, calls=%fused_computation.18 | loop fusion | flops 1486848 | bytes 5947392 | tf_op jit(solution)/shard_map/mul | solution.py:51
  2.8 1.8 %copy-done.7 = bf16[8,1408,352]{1,2,0:T(8,128)(2,1)S(1)} copy-done((bf16[8,1408,352]{1,2,0:T(8,128)(2,1)S(1)}, bf16[8,1408,352]{1,2,0:T(8,128)(2,1)}, u32[]{:S(2)}) %copy-start.7) | copy-done | bytes 7929880
  4.6 3.9 %fusion.27 = bf16[8,176,352]{2,1,0:T(8,128)(2,1)} fusion(bf16[8,1408,352]{1,2,0:T(8,128)(2,1)S(1)} %copy-done.7, bf16[176,1408]{1,0:T(8,128)(2,1)S(1)} %get-tuple-element.78), kind=kOutput, calls=%fused_computation.17 | convolution fusion | flops 1396150272 | bytes 9416704 | tf_op jit(solution)/shard_map/dot_general | solution.py:63
  8.5 6.3 %all-to-all-start.1 = ((bf16[8,176,352]{2,1,0:T(8,128)(2,1)}), bf16[8,176,352]{2,1,0:T(8,128)(2,1)S(1)}, u32[]{:S(2)}, u32[]{:S(2)}) async-start(bf16[8,176,352]{2,1,0:T(8,128)(2,1)} %fusion.27), calls=%async_computation.1 | async-start | bytes 2162688 | tf_op jit(solution)/shard_map/all_to_all | solution.py:75
  14.9 7.2 %fusion.24 = bf16[8,176,352]{2,1,0:T(8,128)(2,1)} fusion(bf16[8,1408,352]{1,2,0:T(8,128)(2,1)} %constant.60.clone, bf16[176,1408]{1,0:T(8,128)(2,1)S(1)} %get-tuple-element.79), kind=kOutput, calls=%fused_computation.16 | convolution fusion | flops 1396150272 | bytes 9416704 | tf_op jit(solution)/shard_map/dot_general | solution.py:63
  22.0 7.2 %fusion.21 = bf16[8,176,352]{2,1,0:T(8,128)(2,1)} fusion(bf16[8,1408,352]{1,2,0:T(8,128)(2,1)} %constant.60.clone, bf16[176,1408]{1,0:T(8,128)(2,1)S(1)} %get-tuple-element.80), kind=kOutput, calls=%fused_computation.15 | convolution fusion | flops 1396150272 | bytes 9416704 | tf_op jit(solution)/shard_map/dot_general | solution.py:63
  29.2 12.9 %all-to-all-done.1 = bf16[8,176,352]{2,1,0:T(8,128)(2,1)S(1)} async-done(((bf16[8,176,352]{2,1,0:T(8,128)(2,1)}), bf16[8,176,352]{2,1,0:T(8,128)(2,1)S(1)}, u32[]{:S(2)}, u32[]{:S(2)}) %all-to-all-start.1) | async-done | bytes 991264 | tf_op jit(solution)/shard_map/all_to_all | solution.py:75
  42.2 3.7 %all-to-all-start = ((bf16[8,176,352]{2,1,0:T(8,128)(2,1)}), bf16[8,176,352]{2,1,0:T(8,128)(2,1)S(1)}, u32[]{:S(2)}, u32[]{:S(2)}) async-start(bf16[8,176,352]{2,1,0:T(8,128)(2,1)} %fusion.24), calls=%async_computation | async-start | bytes 2162688 | tf_op jit(solution)/shard_map/all_to_all | solution.py:75
  46.3 1.3 pad_maximum_fusion.1
  47.6 1.7 copy.7
  49.3 9.3 %fusion.15 = bf16[8,176,352]{2,1,0:T(8,128)(2,1)S(1)} fusion(bf16[8,352,2816]{2,1,0:T(8,128)(2,1)} %constant.61.clone, bf16[2816,176]{0,1:T(8,128)(2,1)S(1)} %copy.7), kind=kOutput, calls=%fused_computation.13 | convolution fusion | flops 2791804928 | bytes 17842176 | tf_op jit(solution)/shard_map/dot_general | solution.py:79
  59.6 1.5 collective-permute-start.3
  61.1 11.9 %all-to-all-done = bf16[8,176,352]{2,1,0:T(8,128)(2,1)S(1)} async-done(((bf16[8,176,352]{2,1,0:T(8,128)(2,1)}), bf16[8,176,352]{2,1,0:T(8,128)(2,1)S(1)}, u32[]{:S(2)}, u32[]{:S(2)}) %all-to-all-start) | async-done | bytes 991264 | tf_op jit(solution)/shard_map/all_to_all | solution.py:75
  73.5 1.5 copy.6
  75.0 9.5 %fusion.12 = bf16[8,176,352]{2,1,0:T(8,128)(2,1)S(1)} fusion(bf16[8,352,2816]{2,1,0:T(8,128)(2,1)} %constant.61.clone, bf16[2816,176]{0,1:T(8,128)(2,1)} %copy.6), kind=kOutput, calls=%fused_computation.12 | convolution fusion | flops 2791804928 | bytes 17842176 | tf_op jit(solution)/shard_map/dot_general | solution.py:79
  84.6 1.6 collective-permute-start
  86.1 1.1 constant_dynamic-slice_fusion.3
  87.2 1.6 collective-permute-start.4
  97.4 4.5 %all-to-all-start.2 = ((bf16[8,176,352]{2,1,0:T(8,128)(2,1)}), bf16[8,176,352]{2,1,0:T(8,128)(2,1)}, u32[]{:S(2)}, u32[]{:S(2)}) async-start(bf16[8,176,352]{2,1,0:T(8,128)(2,1)} %fusion.21), calls=%async_computation.2 | async-start | bytes 2162688 | tf_op jit(solution)/shard_map/all_to_all | solution.py:75
  102.4 1.1 constant_dynamic-slice_fusion.6
  103.5 2.5 %collective-permute-start.2 = (bf16[1,2,352,176]{2,3,1,0:T(8,128)(2,1)S(1)}, bf16[1,2,352,176]{2,3,1,0:T(8,128)(2,1)S(1)}, u32[]{:S(2)}, u32[]{:S(2)}) collective-permute-start(bf16[1,2,352,176]{2,3,1,0:T(8,128)(2,1)S(1)} %get-tuple-element.91), channel_id=1, source_target_pairs={{0,24},{8,16},{16,8},{24,0},{1,25},{9,17},{17,9},{25,1},{2,26},{10... | collective-permute-start | bytes 743432 | tf_op jit(solution)/shard_map/ppermute | solution.py:45
  106.5 5.7 %collective-permute-done.5 = bf16[1,2,352,176]{2,3,1,0:T(8,128)(2,1)S(1)} collective-permute-done((bf16[1,2,352,176]{2,3,1,0:T(8,128)(2,1)S(1)}, bf16[1,2,352,176]{2,3,1,0:T(8,128)(2,1)S(1)}, u32[]{:S(2)}, u32[]{:S(2)}) %collective-permute-start.5) | collective-permute-done | bytes 247840 | tf_op jit(solution)/shard_map/ppermute | solution.py:45
  113.2 9.7 %collective-permute-done.1 = bf16[1,2,352,176]{2,3,1,0:T(8,128)(2,1)S(1)} collective-permute-done((bf16[1,2,352,176]{2,3,1,0:T(8,128)(2,1)S(1)}, bf16[1,2,352,176]{2,3,1,0:T(8,128)(2,1)S(1)}, u32[]{:S(2)}, u32[]{:S(2)}) %collective-permute-start.1) | collective-permute-done | bytes 247840 | tf_op jit(solution)/shard_map/ppermute | solution.py:45
  125.4 3.6 %all-to-all-done.2 = bf16[8,176,352]{2,1,0:T(8,128)(2,1)} async-done(((bf16[8,176,352]{2,1,0:T(8,128)(2,1)}), bf16[8,176,352]{2,1,0:T(8,128)(2,1)}, u32[]{:S(2)}, u32[]{:S(2)}) %all-to-all-start.2) | async-done | bytes 991264 | tf_op jit(solution)/shard_map/all_to_all | solution.py:75
  128.9 1.7 fusion.42
  130.6 1.3 pad_maximum_fusion.2
  131.9 2.4 %copy.8 = bf16[2816,176]{0,1:T(8,128)(2,1)} copy(bf16[2816,176]{1,0:T(8,128)(2,1)} %pad_maximum_fusion.2) | data formatting | bytes 1982464 | tf_op jit(solution)/shard_map/concatenate | solution.py:77
  134.4 9.5 %fusion.18 = bf16[8,176,352]{2,1,0:T(8,128)(2,1)S(1)} fusion(bf16[8,352,2816]{2,1,0:T(8,128)(2,1)} %constant.61.clone, bf16[2816,176]{0,1:T(8,128)(2,1)} %copy.8), kind=kOutput, calls=%fused_computation.14 | convolution fusion | flops 2791804928 | bytes 17842176 | tf_op jit(solution)/shard_map/dot_general | solution.py:79
  144.6 7.4 %collective-permute-done.6 = bf16[1,2,352,176]{2,3,1,0:T(8,128)(2,1)S(1)} collective-permute-done((bf16[1,2,352,176]{2,3,1,0:T(8,128)(2,1)S(1)}, bf16[1,2,352,176]{2,3,1,0:T(8,128)(2,1)S(1)}, u32[]{:S(2)}, u32[]{:S(2)}) %collective-permute-start.6) | collective-permute-done | bytes 247840 | tf_op jit(solution)/shard_map/ppermute | solution.py:45
  152.7 1.5 collective-permute-start.7
  154.3 11.0 %collective-permute-done.7 = bf16[1,2,352,176]{2,3,1,0:T(8,128)(2,1)S(1)} collective-permute-done((bf16[1,2,352,176]{2,3,1,0:T(8,128)(2,1)S(1)}, bf16[1,2,352,176]{2,3,1,0:T(8,128)(2,1)S(1)}, u32[]{:S(2)}, u32[]{:S(2)}) %collective-permute-start.7) | collective-permute-done | bytes 247840 | tf_op jit(solution)/shard_map/ppermute | solution.py:45
  168.0 2.8 %copy-done.5 = f32[24,352,176]{1,2,0:T(8,128)} copy-done((f32[24,352,176]{1,2,0:T(8,128)}, f32[24,352,176]{1,2,0:T(8,128)S(1)}, u32[]{:S(2)}) %copy-start.5) | copy-done | bytes 5947416
  (77 shorter events, 11.1 us)
Async XLA Ops:
  0.0 4.6 %copy-start.7 = (bf16[8,1408,352]{1,2,0:T(8,128)(2,1)S(1)}, bf16[8,1408,352]{1,2,0:T(8,128)(2,1)}, u32[]{:S(2)}) copy-start(bf16[8,1408,352]{1,2,0:T(8,128)(2,1)} %constant.60.clone) | copy-start | bytes 23789572
  8.5 33.6 %all-to-all-start.1 = ((bf16[8,176,352]{2,1,0:T(8,128)(2,1)}), bf16[8,176,352]{2,1,0:T(8,128)(2,1)S(1)}, u32[]{:S(2)}, u32[]{:S(2)}) async-start(bf16[8,176,352]{2,1,0:T(8,128)(2,1)} %fusion.27), calls=%async_computation.1 | async-start | bytes 2162688 | tf_op jit(solution)/shard_map/all_to_all | solution.py:75
  42.2 30.8 %all-to-all-start = ((bf16[8,176,352]{2,1,0:T(8,128)(2,1)}), bf16[8,176,352]{2,1,0:T(8,128)(2,1)S(1)}, u32[]{:S(2)}, u32[]{:S(2)}) async-start(bf16[8,176,352]{2,1,0:T(8,128)(2,1)} %fusion.24), calls=%async_computation | async-start | bytes 2162688 | tf_op jit(solution)/shard_map/all_to_all | solution.py:75
  58.6 1.0 copy-start.3
  59.6 26.6 %collective-permute-start.3 = (bf16[1,2,352,176]{2,3,1,0:T(8,128)(2,1)S(1)}, bf16[1,2,352,176]{2,3,1,0:T(8,128)(2,1)}, u32[]{:S(2)}, u32[]{:S(2)}) collective-permute-start(bf16[1,2,352,176]{2,3,1,0:T(8,128)(2,1)S(1)} %constant_dynamic-slice_fusion.5), channel_id=1, source_target_pairs={{0,8},{8,0},{16,24},{24,16},{1,9},{9,1},{17,25},{25,17},{2,10},{10... | collective-permute-start | bytes 743432 | tf_op jit(solution)/shard_map/ppermute | solution.py:45
  75.0 11.1 %copy-start.4 = (bf16[8,176,352]{2,1,0:T(8,128)(2,1)S(1)}, bf16[8,176,352]{2,1,0:T(8,128)(2,1)}, u32[]{:S(2)}) copy-start(bf16[8,176,352]{2,1,0:T(8,128)(2,1)} %copy-done.3) | copy-start | bytes 2973700
  75.0 13.8 %copy-start.6 = (s32[4]{0:T(128)S(1)}, s32[4]{0:T(128)}, u32[]{:S(2)}) copy-start(s32[4]{0:T(128)} %param.7) | copy-start | bytes 52
  84.6 17.8 %collective-permute-start = (bf16[1,2,352,176]{2,3,1,0:T(8,128)(2,1)S(1)}, bf16[1,2,352,176]{2,3,1,0:T(8,128)(2,1)}, u32[]{:S(2)}, u32[]{:S(2)}) collective-permute-start(bf16[1,2,352,176]{2,3,1,0:T(8,128)(2,1)S(1)} %constant_dynamic-slice_fusion.8), channel_id=1, source_target_pairs={{0,8},{8,0},{16,24},{24,16},{1,9},{9,1},{17,25},{25,17},{2,10},{10... | collective-permute-start | bytes 743432 | tf_op jit(solution)/shard_map/ppermute | solution.py:45
  87.2 19.3 %collective-permute-start.4 = (bf16[1,2,352,176]{2,3,1,0:T(8,128)(2,1)S(1)}, bf16[1,2,352,176]{2,3,1,0:T(8,128)(2,1)S(1)}, u32[]{:S(2)}, u32[]{:S(2)}) collective-permute-start(bf16[1,2,352,176]{2,3,1,0:T(8,128)(2,1)S(1)} %get-tuple-element.87), channel_id=1, source_target_pairs={{0,16},{8,24},{16,0},{24,8},{1,17},{9,25},{17,1},{25,9},{2,18},{10... | collective-permute-start | bytes 743432 | tf_op jit(solution)/shard_map/ppermute | solution.py:45
  97.4 31.6 %all-to-all-start.2 = ((bf16[8,176,352]{2,1,0:T(8,128)(2,1)}), bf16[8,176,352]{2,1,0:T(8,128)(2,1)}, u32[]{:S(2)}, u32[]{:S(2)}) async-start(bf16[8,176,352]{2,1,0:T(8,128)(2,1)} %fusion.21), calls=%async_computation.2 | async-start | bytes 2162688 | tf_op jit(solution)/shard_map/all_to_all | solution.py:75
  101.9 10.4 %collective-permute-start.5 = (bf16[1,2,352,176]{2,3,1,0:T(8,128)(2,1)S(1)}, bf16[1,2,352,176]{2,3,1,0:T(8,128)(2,1)S(1)}, u32[]{:S(2)}, u32[]{:S(2)}) collective-permute-start(bf16[1,2,352,176]{2,3,1,0:T(8,128)(2,1)S(1)} %get-tuple-element.86), channel_id=1, source_target_pairs={{0,24},{8,16},{16,8},{24,0},{1,25},{9,17},{17,9},{25,1},{2,26},{10... | collective-permute-start | bytes 743432 | tf_op jit(solution)/shard_map/ppermute | solution.py:45
  103.5 19.5 %collective-permute-start.2 = (bf16[1,2,352,176]{2,3,1,0:T(8,128)(2,1)S(1)}, bf16[1,2,352,176]{2,3,1,0:T(8,128)(2,1)S(1)}, u32[]{:S(2)}, u32[]{:S(2)}) collective-permute-start(bf16[1,2,352,176]{2,3,1,0:T(8,128)(2,1)S(1)} %get-tuple-element.91), channel_id=1, source_target_pairs={{0,24},{8,16},{16,8},{24,0},{1,25},{9,17},{17,9},{25,1},{2,26},{10... | collective-permute-start | bytes 743432 | tf_op jit(solution)/shard_map/ppermute | solution.py:45
  106.0 16.9 %collective-permute-start.1 = (bf16[1,2,352,176]{2,3,1,0:T(8,128)(2,1)S(1)}, bf16[1,2,352,176]{2,3,1,0:T(8,128)(2,1)S(1)}, u32[]{:S(2)}, u32[]{:S(2)}) collective-permute-start(bf16[1,2,352,176]{2,3,1,0:T(8,128)(2,1)S(1)} %get-tuple-element.92), channel_id=1, source_target_pairs={{0,16},{8,24},{16,0},{24,8},{1,17},{9,25},{17,1},{25,9},{2,18},{10... | collective-permute-start | bytes 743432 | tf_op jit(solution)/shard_map/ppermute | solution.py:45
  134.4 10.1 %copy-start = (f32[352,176]{0,1:T(8,128)S(1)}, f32[352,176]{0,1:T(8,128)}, u32[]{:S(2)}) copy-start(f32[352,176]{0,1:T(8,128)} %get-tuple-element.34) | copy-start | bytes 743428
  134.4 10.1 %copy-start.1 = (f32[352,176]{0,1:T(8,128)S(1)}, f32[352,176]{0,1:T(8,128)}, u32[]{:S(2)}) copy-start(f32[352,176]{0,1:T(8,128)} %get-tuple-element.35) | copy-start | bytes 743428
  134.4 10.1 %copy-start.2 = (f32[352,176]{0,1:T(8,128)S(1)}, f32[352,176]{0,1:T(8,128)}, u32[]{:S(2)}) copy-start(f32[352,176]{0,1:T(8,128)} %get-tuple-element.33) | copy-start | bytes 743428
  143.9 8.1 %collective-permute-start.6 = (bf16[1,2,352,176]{2,3,1,0:T(8,128)(2,1)S(1)}, bf16[1,2,352,176]{2,3,1,0:T(8,128)(2,1)S(1)}, u32[]{:S(2)}, u32[]{:S(2)}) collective-permute-start(bf16[1,2,352,176]{2,3,1,0:T(8,128)(2,1)S(1)} %constant_dynamic-slice_fusion.2), channel_id=1, source_target_pairs={{0,8},{8,0},{16,24},{24,16},{1,9},{9,1},{17,25},{25,17},{2,10},{10... | collective-permute-start | bytes 743432 | tf_op jit(solution)/shard_map/ppermute | solution.py:45
  152.1 13.2 %collective-permute-start.8 = (bf16[1,2,352,176]{2,3,1,0:T(8,128)(2,1)S(1)}, bf16[1,2,352,176]{2,3,1,0:T(8,128)(2,1)S(1)}, u32[]{:S(2)}, u32[]{:S(2)}) collective-permute-start(bf16[1,2,352,176]{2,3,1,0:T(8,128)(2,1)S(1)} %get-tuple-element.81), channel_id=1, source_target_pairs={{0,24},{8,16},{16,8},{24,0},{1,25},{9,17},{17,9},{25,1},{2,26},{10... | collective-permute-start | bytes 743432 | tf_op jit(solution)/shard_map/ppermute | solution.py:45
  152.7 12.6 %collective-permute-start.7 = (bf16[1,2,352,176]{2,3,1,0:T(8,128)(2,1)S(1)}, bf16[1,2,352,176]{2,3,1,0:T(8,128)(2,1)S(1)}, u32[]{:S(2)}, u32[]{:S(2)}) collective-permute-start(bf16[1,2,352,176]{2,3,1,0:T(8,128)(2,1)S(1)} %get-tuple-element.82), channel_id=1, source_target_pairs={{0,16},{8,24},{16,0},{24,8},{1,17},{9,25},{17,1},{25,9},{2,18},{10... | collective-permute-start | bytes 743432 | tf_op jit(solution)/shard_map/ppermute | solution.py:45
  168.0 2.8 %copy-start.5 = (f32[24,352,176]{1,2,0:T(8,128)}, f32[24,352,176]{1,2,0:T(8,128)S(1)}, u32[]{:S(2)}) copy-start(f32[24,352,176]{1,2,0:T(8,128)S(1)} %bitcast_dynamic-update-slice_fusion) | copy-start | bytes 17842180

commit v3 on v2

--- a/solution.py
+++ b/solution.py
@@ -70,8 +70,6 @@
     spectra = []
     for channel in range(channels):
         g = columns[channel]
-        if channel >= 2:
-            g, spectra[channel - 2] = lax.optimization_barrier((g, spectra[channel - 2]))
         g = lax.all_to_all(g, "row", split_axis=0, concat_axis=0, tiled=True)
         g = g.reshape(rows, 2 * cols_here)
         g = jnp.concatenate([g[:, :cols_here], g[:, cols_here:]], axis=0)

time: 171 us -> 162 us (0.947)
  waiting for transfers between devices: 62.3 us -> 58.5 us
  local copies, waits for them, and re-layouts: 16.8 us -> 13.8 us
  other arithmetic: 11.4 us -> 8.81 us
    ppermute x9, waiting for transfers between devices: 33.9 us -> 27.9 us  [to_slot_owners(): arrived = lax.ppermute(block, 'slot', pairs)]
    concatenate x3, local copies, waits for them, and re-layouts: 5.64 us -> 3.14 us  [on_device(): g = jnp.concatenate([g[:, :cols_here], g[:, cols_here:]], axis=0)]
    all_to_all x3, waiting for transfers between devices: 28.4 us -> 30.6 us  [on_device(): g = lax.all_to_all(g, 'row', split_axis=0, concat_axis=0, tiled=True)]
    ppermute x9, starting transfers between devices: 10.8 us -> 12.6 us  [to_slot_owners(): arrived = lax.ppermute(block, 'slot', pairs)]
    unnamed x16 -> x10, local copies, waits for them, and re-layouts: 5.47 us -> 4.79 us
  transfers between devices with their start and end apart: 12 -> 12, of which waited for: 7 -> 6; matrix products, arithmetic and copies ran while one was open for 26% -> 34% of each run, Pallas kernels for 0% -> 0%
where the time goes in v3:
time: 162 us
  waiting for transfers between devices  58.5 us (36%)
  matrix products  46.2 us (29%)
  starting transfers between devices  26.3 us (16%)
  local copies, waits for them, and re-layouts  13.8 us (9%)
  other arithmetic  8.81 us (5%)
  between operations  8.19 us (5%)
    all_to_all x3, waiting for transfers between devices, on_device(): g = lax.all_to_all(g, 'row', split_axis=0, concat_axis=0, tiled=True)  30.6 us
    ppermute x9, waiting for transfers between devices, to_slot_owners(): arrived = lax.ppermute(block, 'slot', pairs)  27.9 us
    dot_general x3, matrix products, on_device(): lax.dot_general(to_rows, g, (((2,), (1,)), ((0,), (0,))), preferred_eleme...  27.9 us
    dot_general x3, matrix products, on_device(): lax.dot_general(spread, to_columns, (((2,), (1,)), ((0,), (0,))), preferr...  18.4 us
    all_to_all x3, starting transfers between devices, on_device(): g = lax.all_to_all(g, 'row', split_axis=0, concat_axis=0, tiled=True)  13.6 us
    ppermute x9, starting transfers between devices, to_slot_owners(): arrived = lax.ppermute(block, 'slot', pairs)  12.6 us
    unnamed x10, local copies, waits for them, and re-layouts  4.79 us
    dynamic_slice x6, local copies, waits for them, and re-layouts, to_slot_owners(): block = lax.dynamic_index_in_dim(spectrum, target, 0, keepdims=True)  3.82 us
  transfers between devices with their start and end apart: 12, of which 6 were waited for; matrix products, arithmetic and copies ran while one was open for 34% of the time, Pallas kernels for 0%

profile of v3, /device:TPU:0, one launch (start us, length us, event | category | flops | bytes accessed | tf_op | source)
XLA Modules:
  0.0 161.8 jit_solution(14967503467687751036)
XLA Ops:
  0.0 2.7 %convert_multiply_fusion = bf16[1,3,176,1408]{3,2,1,0:T(8,128)(2,1)S(1)} fusion(bf16[1,3,176,1408]{3,2,1,0:T(8,128)(2,1)} %param.5, s32[1,3,176,1408]{3,2,1,0:T(8,128)} %param.6), kind=kLoop, calls=%fused_computation.18 | loop fusion | flops 1486848 | bytes 5947392 | tf_op jit(solution)/shard_map/mul | solution.py:51
  2.8 1.8 %copy-done.4 = bf16[8,1408,352]{1,2,0:T(8,128)(2,1)S(1)} copy-done((bf16[8,1408,352]{1,2,0:T(8,128)(2,1)S(1)}, bf16[8,1408,352]{1,2,0:T(8,128)(2,1)}, u32[]{:S(2)}) %copy-start.4) | copy-done | bytes 7929880
  4.6 3.9 %fusion.27 = bf16[8,176,352]{2,1,0:T(8,128)(2,1)} fusion(bf16[8,1408,352]{1,2,0:T(8,128)(2,1)S(1)} %copy-done.4, bf16[176,1408]{1,0:T(8,128)(2,1)S(1)} %get-tuple-element.74), kind=kOutput, calls=%fused_computation.17 | convolution fusion | flops 1396150272 | bytes 9416704 | tf_op jit(solution)/shard_map/dot_general | solution.py:63
  8.5 6.3 %all-to-all-start.2 = ((bf16[8,176,352]{2,1,0:T(8,128)(2,1)}), bf16[8,176,352]{2,1,0:T(8,128)(2,1)S(1)}, u32[]{:S(2)}, u32[]{:S(2)}) async-start(bf16[8,176,352]{2,1,0:T(8,128)(2,1)} %fusion.27), calls=%async_computation.2 | async-start | bytes 2162688 | tf_op jit(solution)/shard_map/all_to_all | solution.py:73
  23.4 7.2 %fusion.24 = bf16[8,176,352]{2,1,0:T(8,128)(2,1)} fusion(bf16[8,1408,352]{1,2,0:T(8,128)(2,1)} %constant.60.clone, bf16[176,1408]{1,0:T(8,128)(2,1)S(1)} %get-tuple-element.75), kind=kOutput, calls=%fused_computation.16 | convolution fusion | flops 1396150272 | bytes 9416704 | tf_op jit(solution)/shard_map/dot_general | solution.py:63
  30.6 7.2 %fusion.21 = bf16[8,176,352]{2,1,0:T(8,128)(2,1)} fusion(bf16[8,1408,352]{1,2,0:T(8,128)(2,1)} %constant.60.clone, bf16[176,1408]{1,0:T(8,128)(2,1)S(1)} %get-tuple-element.76), kind=kOutput, calls=%fused_computation.15 | convolution fusion | flops 1396150272 | bytes 9416704 | tf_op jit(solution)/shard_map/dot_general | solution.py:63
  37.8 4.4 %all-to-all-done.2 = bf16[8,176,352]{2,1,0:T(8,128)(2,1)S(1)} async-done(((bf16[8,176,352]{2,1,0:T(8,128)(2,1)}), bf16[8,176,352]{2,1,0:T(8,128)(2,1)S(1)}, u32[]{:S(2)}, u32[]{:S(2)}) %all-to-all-start.2) | async-done | bytes 991264 | tf_op jit(solution)/shard_map/all_to_all | solution.py:73
  42.2 3.6 %all-to-all-start.1 = ((bf16[8,176,352]{2,1,0:T(8,128)(2,1)}), bf16[8,176,352]{2,1,0:T(8,128)(2,1)S(1)}, u32[]{:S(2)}, u32[]{:S(2)}) async-start(bf16[8,176,352]{2,1,0:T(8,128)(2,1)} %fusion.24), calls=%async_computation.1 | async-start | bytes 2162688 | tf_op jit(solution)/shard_map/all_to_all | solution.py:73
  46.1 1.3 pad_maximum_fusion.2
  47.4 1.7 %copy.8 = bf16[2816,176]{0,1:T(8,128)(2,1)S(1)} copy(bf16[2816,176]{1,0:T(8,128)(2,1)} %pad_maximum_fusion.2) | data formatting | bytes 1982464 | tf_op jit(solution)/shard_map/concatenate | solution.py:75
  49.1 9.3 %fusion.18 = bf16[8,176,352]{2,1,0:T(8,128)(2,1)S(1)} fusion(bf16[8,352,2816]{2,1,0:T(8,128)(2,1)} %constant.61.clone, bf16[2816,176]{0,1:T(8,128)(2,1)S(1)} %copy.8), kind=kOutput, calls=%fused_computation.14 | convolution fusion | flops 2791804928 | bytes 17842176 | tf_op jit(solution)/shard_map/dot_general | solution.py:77
  58.4 0.8 constant_dynamic-slice_fusion.2
  59.5 1.5 collective-permute-start.6
  60.9 12.0 %all-to-all-done.1 = bf16[8,176,352]{2,1,0:T(8,128)(2,1)S(1)} async-done(((bf16[8,176,352]{2,1,0:T(8,128)(2,1)}), bf16[8,176,352]{2,1,0:T(8,128)(2,1)S(1)}, u32[]{:S(2)}, u32[]{:S(2)}) %all-to-all-start.1) | async-done | bytes 991264 | tf_op jit(solution)/shard_map/all_to_all | solution.py:73
  73.0 3.7 %all-to-all-start = ((bf16[8,176,352]{2,1,0:T(8,128)(2,1)}), bf16[8,176,352]{2,1,0:T(8,128)(2,1)S(1)}, u32[]{:S(2)}, u32[]{:S(2)}) async-start(bf16[8,176,352]{2,1,0:T(8,128)(2,1)} %fusion.21), calls=%async_computation | async-start | bytes 2162688 | tf_op jit(solution)/shard_map/all_to_all | solution.py:73
  77.3 0.7 copy.7
  78.0 9.3 %fusion.15 = bf16[8,176,352]{2,1,0:T(8,128)(2,1)S(1)} fusion(bf16[8,352,2816]{2,1,0:T(8,128)(2,1)} %constant.61.clone, bf16[2816,176]{0,1:T(8,128)(2,1)S(1)} %copy.7), kind=kOutput, calls=%fused_computation.13 | convolution fusion | flops 2791804928 | bytes 17842176 | tf_op jit(solution)/shard_map/dot_general | solution.py:77
  87.3 0.7 constant_dynamic-slice_fusion.5
  88.0 1.5 collective-permute-start.3
  89.5 14.2 %all-to-all-done = bf16[8,176,352]{2,1,0:T(8,128)(2,1)S(1)} async-done(((bf16[8,176,352]{2,1,0:T(8,128)(2,1)}), bf16[8,176,352]{2,1,0:T(8,128)(2,1)S(1)}, u32[]{:S(2)}, u32[]{:S(2)}) %all-to-all-start) | async-done | bytes 991264 | tf_op jit(solution)/shard_map/all_to_all | solution.py:73
  104.3 0.7 copy.6
  105.1 9.4 %fusion.12 = bf16[8,176,352]{2,1,0:T(8,128)(2,1)S(1)} fusion(bf16[8,352,2816]{2,1,0:T(8,128)(2,1)} %constant.61.clone, bf16[2816,176]{0,1:T(8,128)(2,1)S(1)} %copy.6), kind=kOutput, calls=%fused_computation.12 | convolution fusion | flops 2791804928 | bytes 17842176 | tf_op jit(solution)/shard_map/dot_general | solution.py:77
  114.5 1.6 collective-permute-start
  116.0 1.1 constant_dynamic-slice_fusion
  117.1 1.6 collective-permute-start.8
  119.2 1.1 constant_dynamic-slice_fusion.3
  120.2 2.5 %collective-permute-start.5 = (bf16[1,2,352,176]{2,3,1,0:T(8,128)(2,1)S(1)}, bf16[1,2,352,176]{2,3,1,0:T(8,128)(2,1)S(1)}, u32[]{:S(2)}, u32[]{:S(2)}) collective-permute-start(bf16[1,2,352,176]{2,3,1,0:T(8,128)(2,1)S(1)} %get-tuple-element.82), channel_id=1, source_target_pairs={{0,24},{8,16},{16,8},{24,0},{1,25},{9,17},{17,9},{25,1},{2,26},{10... | collective-permute-start | bytes 743432 | tf_op jit(solution)/shard_map/ppermute | solution.py:45
  123.3 0.7 collective-permute-done
  124.1 2.5 %collective-permute-start.2 = (bf16[1,2,352,176]{2,3,1,0:T(8,128)(2,1)S(1)}, bf16[1,2,352,176]{2,3,1,0:T(8,128)(2,1)S(1)}, u32[]{:S(2)}, u32[]{:S(2)}) collective-permute-start(bf16[1,2,352,176]{2,3,1,0:T(8,128)(2,1)S(1)} %get-tuple-element.87), channel_id=1, source_target_pairs={{0,24},{8,16},{16,8},{24,0},{1,25},{9,17},{17,9},{25,1},{2,26},{10... | collective-permute-start | bytes 743432 | tf_op jit(solution)/shard_map/ppermute | solution.py:45
  126.6 18.8 %collective-permute-done.7 = bf16[1,2,352,176]{2,3,1,0:T(8,128)(2,1)S(1)} collective-permute-done((bf16[1,2,352,176]{2,3,1,0:T(8,128)(2,1)S(1)}, bf16[1,2,352,176]{2,3,1,0:T(8,128)(2,1)S(1)}, u32[]{:S(2)}, u32[]{:S(2)}) %collective-permute-start.7) | collective-permute-done | bytes 247840 | tf_op jit(solution)/shard_map/ppermute | solution.py:45
  146.7 8.4 %collective-permute-done.1 = bf16[1,2,352,176]{2,3,1,0:T(8,128)(2,1)S(1)} collective-permute-done((bf16[1,2,352,176]{2,3,1,0:T(8,128)(2,1)S(1)}, bf16[1,2,352,176]{2,3,1,0:T(8,128)(2,1)S(1)}, u32[]{:S(2)}, u32[]{:S(2)}) %collective-permute-start.1) | collective-permute-done | bytes 247840 | tf_op jit(solution)/shard_map/ppermute | solution.py:45
  159.1 2.8 %copy-done.2 = f32[24,352,176]{1,2,0:T(8,128)} copy-done((f32[24,352,176]{1,2,0:T(8,128)}, f32[24,352,176]{1,2,0:T(8,128)S(1)}, u32[]{:S(2)}) %copy-start.2) | copy-done | bytes 5947416
  (71 shorter events, 8.8 us)
Async XLA Ops:
  0.0 4.6 %copy-start.4 = (bf16[8,1408,352]{1,2,0:T(8,128)(2,1)S(1)}, bf16[8,1408,352]{1,2,0:T(8,128)(2,1)}, u32[]{:S(2)}) copy-start(bf16[8,1408,352]{1,2,0:T(8,128)(2,1)} %constant.60.clone) | copy-start | bytes 23789572
  4.6 10.3 %copy-start.3 = (s32[4]{0:T(128)S(1)}, s32[4]{0:T(128)}, u32[]{:S(2)}) copy-start(s32[4]{0:T(128)} %param.7) | copy-start | bytes 52
  8.5 33.6 %all-to-all-start.2 = ((bf16[8,176,352]{2,1,0:T(8,128)(2,1)}), bf16[8,176,352]{2,1,0:T(8,128)(2,1)S(1)}, u32[]{:S(2)}, u32[]{:S(2)}) async-start(bf16[8,176,352]{2,1,0:T(8,128)(2,1)} %fusion.27), calls=%async_computation.2 | async-start | bytes 2162688 | tf_op jit(solution)/shard_map/all_to_all | solution.py:73
  42.2 30.8 %all-to-all-start.1 = ((bf16[8,176,352]{2,1,0:T(8,128)(2,1)}), bf16[8,176,352]{2,1,0:T(8,128)(2,1)S(1)}, u32[]{:S(2)}, u32[]{:S(2)}) async-start(bf16[8,176,352]{2,1,0:T(8,128)(2,1)} %fusion.24), calls=%async_computation.1 | async-start | bytes 2162688 | tf_op jit(solution)/shard_map/all_to_all | solution.py:73
  58.4 1.1 copy-start
  59.5 56.6 %collective-permute-start.6 = (bf16[1,2,352,176]{2,3,1,0:T(8,128)(2,1)}, bf16[1,2,352,176]{2,3,1,0:T(8,128)(2,1)}, u32[]{:S(2)}, u32[]{:S(2)}) collective-permute-start(bf16[1,2,352,176]{2,3,1,0:T(8,128)(2,1)} %constant_dynamic-slice_fusion.2), channel_id=1, source_target_pairs={{0,8},{8,0},{16,24},{24,16},{1,9},{9,1},{17,25},{25,17},{2,10},{10... | collective-permute-start | bytes 743432 | tf_op jit(solution)/shard_map/ppermute | solution.py:45
  73.0 30.8 %all-to-all-start = ((bf16[8,176,352]{2,1,0:T(8,128)(2,1)}), bf16[8,176,352]{2,1,0:T(8,128)(2,1)S(1)}, u32[]{:S(2)}, u32[]{:S(2)}) async-start(bf16[8,176,352]{2,1,0:T(8,128)(2,1)} %fusion.21), calls=%async_computation | async-start | bytes 2162688 | tf_op jit(solution)/shard_map/all_to_all | solution.py:73
  88.0 31.2 %collective-permute-start.3 = (bf16[1,2,352,176]{2,3,1,0:T(8,128)(2,1)}, bf16[1,2,352,176]{2,3,1,0:T(8,128)(2,1)}, u32[]{:S(2)}, u32[]{:S(2)}) collective-permute-start(bf16[1,2,352,176]{2,3,1,0:T(8,128)(2,1)} %constant_dynamic-slice_fusion.5), channel_id=1, source_target_pairs={{0,8},{8,0},{16,24},{24,16},{1,9},{9,1},{17,25},{25,17},{2,10},{10... | collective-permute-start | bytes 743432 | tf_op jit(solution)/shard_map/ppermute | solution.py:45
  105.0 11.0 %copy-start.1 = (bf16[8,176,352]{2,1,0:T(8,128)(2,1)S(1)}, bf16[8,176,352]{2,1,0:T(8,128)(2,1)}, u32[]{:S(2)}) copy-start(bf16[8,176,352]{2,1,0:T(8,128)(2,1)} %copy-done) | copy-start | bytes 2973700
  114.5 9.5 %collective-permute-start = (bf16[1,2,352,176]{2,3,1,0:T(8,128)(2,1)S(1)}, bf16[1,2,352,176]{2,3,1,0:T(8,128)(2,1)S(1)}, u32[]{:S(2)}, u32[]{:S(2)}) collective-permute-start(bf16[1,2,352,176]{2,3,1,0:T(8,128)(2,1)S(1)} %constant_dynamic-slice_fusion.8), channel_id=1, source_target_pairs={{0,8},{8,0},{16,24},{24,16},{1,9},{9,1},{17,25},{25,17},{2,10},{10... | collective-permute-start | bytes 743432 | tf_op jit(solution)/shard_map/ppermute | solution.py:45
  117.1 28.9 %collective-permute-start.8 = (bf16[1,2,352,176]{2,3,1,0:T(8,128)(2,1)S(1)}, bf16[1,2,352,176]{2,3,1,0:T(8,128)(2,1)S(1)}, u32[]{:S(2)}, u32[]{:S(2)}) collective-permute-start(bf16[1,2,352,176]{2,3,1,0:T(8,128)(2,1)S(1)} %get-tuple-element.77), channel_id=1, source_target_pairs={{0,24},{8,16},{16,8},{24,0},{1,25},{9,17},{17,9},{25,1},{2,26},{10... | collective-permute-start | bytes 743432 | tf_op jit(solution)/shard_map/ppermute | solution.py:45
  118.7 26.7 %collective-permute-start.7 = (bf16[1,2,352,176]{2,3,1,0:T(8,128)(2,1)S(1)}, bf16[1,2,352,176]{2,3,1,0:T(8,128)(2,1)S(1)}, u32[]{:S(2)}, u32[]{:S(2)}) collective-permute-start(bf16[1,2,352,176]{2,3,1,0:T(8,128)(2,1)S(1)} %get-tuple-element.78), channel_id=1, source_target_pairs={{0,16},{8,24},{16,0},{24,8},{1,17},{9,25},{17,1},{25,9},{2,18},{10... | collective-permute-start | bytes 743432 | tf_op jit(solution)/shard_map/ppermute | solution.py:45
  120.2 36.1 %collective-permute-start.5 = (bf16[1,2,352,176]{2,3,1,0:T(8,128)(2,1)S(1)}, bf16[1,2,352,176]{2,3,1,0:T(8,128)(2,1)S(1)}, u32[]{:S(2)}, u32[]{:S(2)}) collective-permute-start(bf16[1,2,352,176]{2,3,1,0:T(8,128)(2,1)S(1)} %get-tuple-element.82), channel_id=1, source_target_pairs={{0,24},{8,16},{16,8},{24,0},{1,25},{9,17},{17,9},{25,1},{2,26},{10... | collective-permute-start | bytes 743432 | tf_op jit(solution)/shard_map/ppermute | solution.py:45
  122.7 33.3 %collective-permute-start.4 = (bf16[1,2,352,176]{2,3,1,0:T(8,128)(2,1)S(1)}, bf16[1,2,352,176]{2,3,1,0:T(8,128)(2,1)S(1)}, u32[]{:S(2)}, u32[]{:S(2)}) collective-permute-start(bf16[1,2,352,176]{2,3,1,0:T(8,128)(2,1)S(1)} %get-tuple-element.83), channel_id=1, source_target_pairs={{0,16},{8,24},{16,0},{24,8},{1,17},{9,25},{17,1},{25,9},{2,18},{10... | collective-permute-start | bytes 743432 | tf_op jit(solution)/shard_map/ppermute | solution.py:45
  124.1 31.3 %collective-permute-start.2 = (bf16[1,2,352,176]{2,3,1,0:T(8,128)(2,1)S(1)}, bf16[1,2,352,176]{2,3,1,0:T(8,128)(2,1)S(1)}, u32[]{:S(2)}, u32[]{:S(2)}) collective-permute-start(bf16[1,2,352,176]{2,3,1,0:T(8,128)(2,1)S(1)} %get-tuple-element.87), channel_id=1, source_target_pairs={{0,24},{8,16},{16,8},{24,0},{1,25},{9,17},{17,9},{25,1},{2,26},{10... | collective-permute-start | bytes 743432 | tf_op jit(solution)/shard_map/ppermute | solution.py:45
  145.4 9.7 %collective-permute-start.1 = (bf16[1,2,352,176]{2,3,1,0:T(8,128)(2,1)S(1)}, bf16[1,2,352,176]{2,3,1,0:T(8,128)(2,1)S(1)}, u32[]{:S(2)}, u32[]{:S(2)}) collective-permute-start(bf16[1,2,352,176]{2,3,1,0:T(8,128)(2,1)S(1)} %get-tuple-element.88), channel_id=1, source_target_pairs={{0,16},{8,24},{16,0},{24,8},{1,17},{9,25},{17,1},{25,9},{2,18},{10... | collective-permute-start | bytes 743432 | tf_op jit(solution)/shard_map/ppermute | solution.py:45
  159.1 2.8 %copy-start.2 = (f32[24,352,176]{1,2,0:T(8,128)}, f32[24,352,176]{1,2,0:T(8,128)S(1)}, u32[]{:S(2)}) copy-start(f32[24,352,176]{1,2,0:T(8,128)S(1)} %bitcast_dynamic-update-slice_fusion) | copy-start | bytes 17842180
